TPU v7x, 256 devices: a whole 4x4x8 slice. The times are simulated.
256 devices in a mesh: dp: 32 (over x, y, core), proto: 8 (over z).
Axes of the slice: x: 4, y: 4, z: 8, core: 2. Of those that a mesh axis runs over, the one named last changes fastest.
Arguments:
- teacher_feat: bfloat16 [16384, 256], P('dp'), may hold values from -6 to 6
- student_feat: bfloat16 [16384, 256], P('dp'), may hold values from -6 to 6
- teacher_protos: bfloat16 [256, 65536], P(None, 'proto'), may hold values from -0.5 to 0.5
- student_protos: bfloat16 [256, 65536], P(None, 'proto'), may hold values from -0.375 to 0.375
Outputs:
- bottleneck_grad: float32 [16384, 256], P('dp')
- proto_grad: float32 [256, 65536], P('dp', 'proto')
All inputs are finite; a program needn't handle non-finite values.
Results may differ from a plain program's by a relative error of at most 0.00065.
The roundings to bfloat16 on the way count: a program that leaves them out, or rounds other values in their place, can miss the bound.
Values may be sent and summed in bfloat16 or wider, within the bound.
A program may use at most 128 MiB of HBM per device.

v0:
```python
import jax
import jax.numpy as jnp
from jax import lax
from jax.sharding import PartitionSpec as P

ITERS = 3
LOSS_SCALE = 256


def unit_rows(x):
    x32 = x.astype(jnp.float32)
    return x32 / jnp.sqrt(jnp.sum(x32 * x32, axis=-1, keepdims=True) + 1e-06)


def unit_columns(w):
    w32 = w.astype(jnp.float32)
    return w32 / jnp.sqrt(jnp.sum(w32 * w32, axis=0, keepdims=True) + 1e-06)


def crop_contract(left, right):
    return lax.dot_general(
        left, right, (((0,), (0,)), ((), ())), preferred_element_type=jnp.float32
    )


def body(teacher_feat, student_feat, teacher_protos, student_protos):
    crops_all = teacher_feat.shape[0] * lax.axis_size("dp")
    protos_all = teacher_protos.shape[1] * lax.axis_size("proto")
    teacher_unit = unit_rows(teacher_feat).astype(jnp.bfloat16)
    teacher_wunit = unit_columns(teacher_protos).astype(jnp.bfloat16)
    s32 = student_feat.astype(jnp.float32)
    student_norm = jnp.sqrt(jnp.sum(s32 * s32, axis=-1, keepdims=True) + 1e-06)
    student_unit32 = s32 / student_norm
    student_unit = student_unit32.astype(jnp.bfloat16)
    student_wunit = unit_columns(student_protos).astype(jnp.bfloat16)
    expo = jnp.exp(jnp.dot(teacher_unit, teacher_wunit, preferred_element_type=jnp.float32) / 0.05)
    sexp = jnp.exp(jnp.dot(student_unit, student_wunit, preferred_element_type=jnp.float32) / 0.1)
    student_part = jnp.sum(sexp, axis=1)
    crop_scale = jnp.ones((expo.shape[0],), jnp.float32)
    row_mass = crop_scale
    proto_scale = jnp.ones((expo.shape[1],), jnp.float32)
    for step in range(ITERS):
        column_mass = lax.psum(jnp.sum(expo * crop_scale[:, None], axis=0), "dp")
        proto_scale = 1.0 / (protos_all * column_mass)
        row_part = jnp.sum(expo * proto_scale[None, :], axis=1)
        row_mass = lax.psum(row_part, "proto")
        crop_scale = 1.0 / (crops_all * row_mass)
    student_sum = lax.psum(student_part, "proto")
    targets = expo * proto_scale[None, :] / row_mass[:, None]
    probs = sexp / student_sum[:, None]
    scores_grad = (LOSS_SCALE / 0.1 * (probs - targets)).astype(jnp.bfloat16)
    unit_part = lax.dot_general(
        scores_grad, student_wunit, (((1,), (1,)), ((), ())), preferred_element_type=jnp.float32
    )
    unit_grad = lax.psum(unit_part, "proto")
    along = jnp.sum(student_unit32 * unit_grad, axis=-1, keepdims=True)
    bottleneck_grad = (unit_grad - student_unit32 * along) / student_norm
    proto_grad = lax.psum_scatter(
        crop_contract(student_unit, scores_grad), "dp", scatter_dimension=0, tiled=True
    )
    return (bottleneck_grad, proto_grad)


def solution(mesh):
    placed = (P("dp", None), P("dp", None), P(None, "proto"), P(None, "proto"))
    return jax.shard_map(
        body,
        mesh=mesh,
        in_specs=placed,
        out_specs=(P("dp", None), P("dp", "proto")),
        check_vma=False,
    )
```

profile of v0, /device:TPU:1, one launch (start us, length us, event | category | flops | bytes accessed | tf_op | source)
XLA Modules:
  0.0 630.8 jit_solution(17086758260261450600)
XLA Ops:
  8.0 0.0 all-reduce.3.cloned.1.call-start
  8.0 1.1 fusion.8
  9.2 1.1 fusion.7
  10.3 3.1 fusion.3
  13.4 3.1 fusion.1
  16.4 11.5 %fusion.19 = (f32[8192]{0:T(1024)S(1)}, f32[512,8192]{1,0:T(8,128)}) fusion(bf16[256,8192]{1,0:T(8,128)(2,1)} %param.6, f32[8192]{0:T(1024)S(1)} %add_sqrt_fusion, bf16[512,256]{1,0:T(8,128)(2,1)} %param.4, f32[512]{0:T(512)S(1)} %add_sqrt_fusion.2), kind=kOutput, calls=%fused_computation.42 | convolution fusion | flops 2162548736 | bytes 21301248 | tf_op jit(solution)/shard_map/dot_general | solution.py:36
  28.0 124.2 %psum.57 = f32[8192]{0:T(1024)S(1)} all-reduce(f32[8192]{0:T(1024)S(1)} %get-tuple-element.4), channel_id=1, replica_groups=mesh['dp'=32,'proto'=8] {'dp'}, use_global_device_ids=true, to_apply=%region_7.0 | all-reduce | flops 8192 | bytes 65536 | tf_op jit(solution)/shard_map/psum | solution.py:43
  152.2 7.3 %multiply_reduce_fusion.3 = f32[512]{0:T(512)S(1)} fusion(f32[512,8192]{1,0:T(8,128)} %get-tuple-element.5, f32[8192]{0:T(1024)S(1)} %multiply_divide_fusion.2), kind=kLoop, calls=%fused_computation.4 | loop fusion | flops 8388096 | bytes 16812032 | tf_op jit(solution)/shard_map/reduce_sum | solution.py:45
  159.5 16.2 %psum.58 = f32[512]{0:T(512)S(1)} all-reduce(f32[512]{0:T(512)S(1)} %multiply_reduce_fusion.3), channel_id=1, replica_groups=mesh['dp'=32,'proto'=8] {'proto'}, use_global_device_ids=true, to_apply=%region_9.0 | all-reduce | flops 512 | bytes 4096 | tf_op jit(solution)/shard_map/psum | solution.py:46
  175.7 8.3 %multiply_reduce_fusion.2 = f32[8192]{0:T(1024)S(1)} fusion(f32[512,8192]{1,0:T(8,128)} %get-tuple-element.5, f32[512]{0:T(512)S(1)} %multiply_divide_fusion.4), kind=kLoop, calls=%fused_computation.3 | loop fusion | flops 8380416 | bytes 16812032 | tf_op jit(solution)/shard_map/reduce_sum | solution.py:43
  184.0 127.5 %psum.59 = f32[8192]{0:T(1024)S(1)} all-reduce(f32[8192]{0:T(1024)S(1)} %multiply_reduce_fusion.2), channel_id=1, replica_groups=mesh['dp'=32,'proto'=8] {'dp'}, use_global_device_ids=true, to_apply=%region_11.0 | all-reduce | flops 8192 | bytes 65536 | tf_op jit(solution)/shard_map/psum | solution.py:43
  311.6 7.3 %multiply_reduce_fusion.1 = f32[512]{0:T(512)S(1)} fusion(f32[512,8192]{1,0:T(8,128)} %get-tuple-element.5, f32[8192]{0:T(1024)S(1)} %multiply_divide_fusion.1), kind=kLoop, calls=%fused_computation.2 | loop fusion | flops 8388096 | bytes 16812032 | tf_op jit(solution)/shard_map/reduce_sum | solution.py:45
  318.8 10.9 %psum.60 = f32[512]{0:T(512)S(1)} all-reduce(f32[512]{0:T(512)S(1)} %multiply_reduce_fusion.1), channel_id=1, replica_groups=mesh['dp'=32,'proto'=8] {'proto'}, use_global_device_ids=true, to_apply=%region_13.0 | all-reduce | flops 512 | bytes 4096 | tf_op jit(solution)/shard_map/psum | solution.py:46
  329.7 8.3 %multiply_reduce_fusion = f32[8192]{0:T(1024)S(1)} fusion(f32[512,8192]{1,0:T(8,128)} %get-tuple-element.5, f32[512]{0:T(512)S(1)} %multiply_divide_fusion.3), kind=kLoop, calls=%fused_computation.1 | loop fusion | flops 8380416 | bytes 16812032 | tf_op jit(solution)/shard_map/reduce_sum | solution.py:43
  338.1 127.2 %psum.61 = f32[8192]{0:T(1024)S(1)} all-reduce(f32[8192]{0:T(1024)S(1)} %multiply_reduce_fusion), channel_id=1, replica_groups=mesh['dp'=32,'proto'=8] {'dp'}, use_global_device_ids=true, to_apply=%region_15.0 | all-reduce | flops 8192 | bytes 65536 | tf_op jit(solution)/shard_map/psum | solution.py:43
  465.3 7.0 %multiply_reduce_fusion.4 = f32[512]{0:T(512)S(1)} fusion(f32[512,8192]{1,0:T(8,128)} %get-tuple-element.5, f32[8192]{0:T(1024)S(1)} %multiply_divide_fusion), kind=kLoop, calls=%fused_computation.7 | loop fusion | flops 8388096 | bytes 16812032 | tf_op jit(solution)/shard_map/reduce_sum | solution.py:45
  472.3 0.0 copy-done.1
  472.3 10.2 %fusion = (f32[512]{0:T(512)S(1)}, f32[512,8192]{1,0:T(8,128)}) fusion(bf16[256,8192]{1,0:T(8,128)(2,1)} %param.7, f32[8192]{0:T(1024)S(1)} %add_sqrt_fusion.1, f32[512]{0:T(512)S(1)} %add_sqrt_fusion.3, bf16[512,256]{1,0:T(8,128)(2,1)S(1)} %copy-done.1), kind=kOutput, calls=%fused_computation.8 | convolution fusion | flops 2162556416 | bytes 21270528 | tf_op jit(solution)/shard_map/dot_general | solution.py:37
  482.5 12.4 %all-reduce = (f32[512]{0:T(512)S(1)}, f32[512]{0:T(512)S(1)}) all-reduce(f32[512]{0:T(512)S(1)} %multiply_reduce_fusion.4, f32[512]{0:T(512)S(1)} %get-tuple-element.6), channel_id=1, replica_groups=mesh['dp'=32,'proto'=8] {'proto'}, use_global_device_ids=true, to_apply=%region_17.0 | all-reduce | flops 1024 | bytes 8192 | tf_op jit(solution)/shard_map/psum | solution.py:46
  494.9 12.2 %multiply_convert_fusion = bf16[512,8192]{1,0:T(8,128)(2,1)S(1)} fusion(f32[512,8192]{1,0:T(8,128)} %get-tuple-element.5, f32[512,8192]{1,0:T(8,128)} %get-tuple-element.7, f32[512]{0:T(512)S(1)} %get-tuple-element.2, f32[8192]{0:T(1024)S(1)} %multiply_divide_fusion, f32[512]{0:T(512)S(1)} %get-tuple-element.3), kind=kLoop, calls=%fused_computation | loop fusion | flops 29360128 | bytes 41979904 | tf_op jit(solution)/shard_map/convert_element_type | solution.py:51
  507.1 0.0 copy-start
  507.1 3.2 copy-done
  510.3 0.0 copy-done.2
  510.3 3.2 fusion.16
  513.5 0.0 all-reduce.3.cloned.1.call-update
  513.5 0.3 reduce-scatter.2.cloned.1.call-start
  513.8 9.1 %fusion.12 = f32[256,8192]{1,0:T(8,128)} fusion(bf16[512,8192]{1,0:T(8,128)(2,1)} %copy-done, bf16[512,256]{1,0:T(8,128)(2,1)S(1)} %copy-done.1, f32[512]{0:T(512)S(1)} %add_sqrt_fusion.3), kind=kOutput, calls=%fused_computation.28 | convolution fusion | flops 2147876864 | bytes 17041408 | tf_op jit(solution)/shard_map/dot_general | solution.py:21
  522.9 0.0 reduce-scatter.2.cloned.1.call-update
  522.9 61.5 %all-reduce.3.cloned.1.call-done = f32[512,256]{1,0:T(8,128)} async-done(((f32[512,256]{1,0:T(8,128)}), f32[512,256]{1,0:T(8,128)}) %all-reduce.3.cloned.1.call-update) | async-done | bytes 524304 | tf_op jit(solution)/shard_map/psum | solution.py:55
  584.4 1.3 multiply_reduce_fusion.5
  585.7 2.1 subtract_divide_fusion
  587.8 35.6 %reduce-scatter.2.cloned.1.call-done = f32[8,8192]{1,0:T(8,128)} async-done(((f32[256,8192]{1,0:T(8,128)}), f32[8,8192]{1,0:T(8,128)}) %reduce-scatter.2.cloned.1.call-update) | async-done | bytes 262160 | tf_op jit(solution)/shard_map/reduce_scatter | solution.py:58
  (11 shorter events, 0.1 us)
Async XLA Ops:
  8.0 576.5 %all-reduce.3.cloned.1.call-start = ((), (), s32[]{:S(2)}) async-start(), calls=%async_computation.1 | async-start | bytes 1048576 | tf_op jit(solution)/shard_map/psum | solution.py:55
  329.7 142.6 %copy-start.1 = (bf16[512,256]{1,0:T(8,128)(2,1)S(1)}, bf16[512,256]{1,0:T(8,128)(2,1)}, u32[]{:S(2)}) copy-start(bf16[512,256]{1,0:T(8,128)(2,1)} %param.5) | copy-start | bytes 786436
  494.9 15.5 %copy-start.2 = (bf16[256,8192]{1,0:T(8,128)(2,1)S(1)}, bf16[256,8192]{1,0:T(8,128)(2,1)}, u32[]{:S(2)}) copy-start(bf16[256,8192]{1,0:T(8,128)(2,1)} %param.7) | copy-start | bytes 12582916
  507.1 3.2 copy-start
  513.5 109.8 %reduce-scatter.2.cloned.1.call-start = ((), (), s32[]{:S(2)}) async-start(), calls=%async_computation.2 | async-start | bytes 8650752 | tf_op jit(solution)/shard_map/reduce_scatter | solution.py:58
Sparse Core Ops, SparseCore 0:
  513.7 70.7 all-reduce.2
Sparse Core Ops, SparseCore 1:
  523.0 100.3 reduce-scatter.1
where the time goes:
time: 632 us; the launch traced here: 631 us
  blocking collectives  418 us (66%)
  waiting for transfers between devices  97.1 us (15%)
  other arithmetic  62.2 us (10%)
  matrix products  33.9 us (5%)
  between operations  15.6 us (2%)
    psum x3, blocking collectives, body(): column_mass = lax.psum(jnp.sum(expo * crop_scale[:, None], axis=0), 'dp')  379 us
    psum x1, waiting for transfers between devices, body(): unit_grad = lax.psum(unit_part, 'proto')  61.5 us
    psum x3, blocking collectives, body(): row_mass = lax.psum(row_part, 'proto')  39.5 us
    reduce_scatter x1, waiting for transfers between devices, body(): lax.psum_scatter(crop_contract(student_unit, scores_grad), 'dp', scatter_...  35.6 us
    reduce_sum x3, other arithmetic, body(): row_part = jnp.sum(expo * proto_scale[None, :], axis=1)  21.5 us
    reduce_sum x2, other arithmetic, body(): column_mass = lax.psum(jnp.sum(expo * crop_scale[:, None], axis=0), 'dp')  16.6 us
  transfers between devices with their start and end apart: 2, of which 2 were waited for; matrix products, arithmetic and copies ran while one was open for 2% of the time, Pallas kernels for 0%

commit v1 on v0

v1 whole, which is shorter than its diff:
```python
import functools
import math

import jax
import jax.numpy as jnp
from jax import lax
from jax.experimental import pallas as pl
from jax.experimental.pallas import tpu as pltpu
from jax.sharding import PartitionSpec as P

F32 = jnp.float32
BF16 = jnp.bfloat16
MESH = pl.DeviceIdType.MESH
ITERS = 3
GRAD_SCALE = 256 / 0.1
TEACHER_RATE = math.log2(math.e) / 0.05
STUDENT_RATE = math.log2(math.e) / 0.1
EPS = 1e-06
NX, NY, NZ = 4, 4, 8
CHIPS = NX * NY
W = 512


def unit_rows(x):
    return x / jnp.sqrt(jnp.sum(x * x, axis=-1, keepdims=True) + EPS)


def kernel(
    crops_all,
    protos_all,
    tf_hbm,
    sf_hbm,
    tw_hbm,
    sw_hbm,
    bout,
    pout,
    tf,
    sf,
    tw,
    sw,
    expo,
    sexp,
    tunit,
    sunit,
    sturn,
    smass,
    rmass,
    rscale,
    ascale,
    bscale,
    pscale,
    colpart,
    corecol,
    colsend,
    colall,
    pvec,
    rowsend,
    rowall,
    scores,
    unit_acc,
    gsend,
    gown,
    grecv,
    hold,
    land1,
    hold2,
    land2,
    unit_in,
    bres,
    ball,
    load_sem,
    feat_sem,
    cc_send,
    cc_recv,
    ca_send,
    ca_recv,
    pv_send,
    pv_recv,
    rw_send,
    rw_recv,
    g_send,
    g_recv,
    l1_send,
    l1_recv,
    l2_send,
    l2_recv,
    u_send,
    u_recv,
    b_send,
    b_recv,
):
    rows, depth = tf.shape
    width = tw.shape[1]
    half = width // 2
    steps = width // W
    hw = W // 2
    d = lax.axis_index("dp")
    z = lax.axis_index("proto")
    core = lax.rem(d, 2)
    chip = lax.div(d, 2)
    x = lax.div(chip, NY)
    y = lax.rem(chip, NY)

    def at(px, py, pc):
        return {"dp": (px * NY + py) * 2 + pc}

    mate = at(x, y, 1 - core)
    chip_peers = []
    for k in range(1, CHIPS):
        px, py = lax.rem(x + k // NY, NX), lax.rem(y + k % NY, NY)
        chip_peers.append((px * NY + py, at(px, py, core)))
    z_peers = [lax.rem(z + k, NZ) for k in range(1, NZ)]

    loads = []
    for i, (src, dst) in enumerate(((tf_hbm, tf), (sf_hbm, sf))):
        c = pltpu.make_async_copy(src, dst, feat_sem.at[i])
        c.start()
        loads.append(c)

    def load(which, src, dst, t):
        cols = pl.ds(pl.multiple_of(t * 2 * W, 2 * W), 2 * W)
        return pltpu.make_async_copy(src.at[:, cols], dst.at[:, cols], load_sem.at[which, t])

    for t in range(steps // 2):
        load(0, tw_hbm, tw, t).start()
    for t in range(steps // 2):
        load(1, sw_hbm, sw, t).start()

    barrier = pltpu.get_barrier_semaphore()
    pl.semaphore_signal(barrier, inc=1, device_id=mate, device_id_type=MESH)
    for _, dev in chip_peers:
        pl.semaphore_signal(barrier, inc=1, device_id=dev, device_id_type=MESH)
    for pz in z_peers:
        pl.semaphore_signal(barrier, inc=1, device_id={"proto": pz}, device_id_type=MESH)

    def normalize(ref, t):
        cols = pl.ds(pl.multiple_of(t * W, W), W)
        w32 = ref[:, cols].astype(F32)
        inv = 1.0 / jnp.sqrt(jnp.sum(w32 * w32, axis=0, keepdims=True) + EPS)
        ref[:, cols] = (w32 * inv).astype(BF16)

    def teacher(t, _):
        @pl.when(lax.rem(t, 2) == 0)
        def _():
            load(0, tw_hbm, tw, lax.div(t, 2)).wait()

        normalize(tw, t)
        cols = pl.ds(pl.multiple_of(t * W, W), W)
        acc = jnp.zeros((8, W), F32)
        for rb in range(rows // 128):
            rs = slice(rb * 128, rb * 128 + 128)
            e = jnp.exp2(jnp.dot(tunit[rs, :], tw[:, cols], preferred_element_type=F32) * TEACHER_RATE)
            expo[rs, cols] = e
            acc = acc + jnp.sum(e.reshape(16, 8, W), axis=0)
        off = pl.ds(pl.multiple_of(lax.rem(t, steps // 2) * W, W), W)
        colpart[lax.div(t, steps // 2), :, off] = jnp.sum(acc, axis=0, keepdims=True)
        return 0

    def student(t, _):
        @pl.when(lax.rem(t, 2) == 0)
        def _():
            load(1, sw_hbm, sw, lax.div(t, 2)).wait()

        normalize(sw, t)
        cols = pl.ds(pl.multiple_of(t * W, W), W)
        for rb in range(rows // 128):
            rs = slice(rb * 128, rb * 128 + 128)
            e = jnp.exp2(jnp.dot(sunit[rs, :], sw[:, cols], preferred_element_type=F32) * STUDENT_RATE)
            sexp[rs, cols] = e
            acc = smass[rs, :]
            for k in range(W // 128):
                acc = acc + e[:, k * 128 : (k + 1) * 128]
            smass[rs, :] = acc
        return 0

    def row_pass():
        def block(i, _):
            rs = pl.ds(pl.multiple_of(i * 64, 64), 64)

            def part(j, acc):
                for k in range(8):
                    cs = pl.ds(pl.multiple_of(j * 1024 + k * 128, 128), 128)
                    e = expo[rs, cs].reshape(8, 8, 128)
                    acc = acc + e * pscale[:, cs][None]
                return acc

            acc = lax.fori_loop(0, width // 1024, part, jnp.zeros((8, 8, 128), F32))
            rmass[rs, :] = acc.reshape(64, 128)
            return 0

        lax.fori_loop(0, rows // 64, block, 0)

    def col_pass():
        def block(j, _):
            def part(i, accs):
                for g in range(8):
                    rs = pl.ds(pl.multiple_of(i * 64 + g * 8, 8), 8)
                    r = rscale[rs, :]
                    accs = tuple(
                        a + expo[rs, pl.ds(pl.multiple_of(j * 1024 + k * 128, 128), 128)] * r
                        for k, a in enumerate(accs)
                    )
                return accs

            accs = lax.fori_loop(0, rows // 64, part, (jnp.zeros((8, 128), F32),) * 8)
            for k in range(8):
                off = lax.rem(j, 4) * 1024 + k * 128
                colpart[lax.div(j, 4), :, pl.ds(pl.multiple_of(off, 128), 128)] = jnp.sum(
                    accs[k], axis=0, keepdims=True
                )
            return 0

        lax.fori_loop(0, width // 1024, block, 0)

    def lane_total(acc):
        return jnp.sum(acc.T, axis=0, keepdims=True)

    def down(vec):
        return jnp.broadcast_to(vec, (128, rows)).T

    def core_copy(it):
        return pltpu.make_async_remote_copy(
            colpart.at[1 - core], corecol.at[it], cc_send.at[it], cc_recv.at[it], mate, MESH
        )

    def col_copy(it, i, arriving):
        q, dev = chip_peers[i]
        q = q if arriving else chip
        return pltpu.make_async_remote_copy(
            colsend.at[it], colall.at[it, q], ca_send.at[it, i], ca_recv.at[it, q], dev, MESH
        )

    def pv_copy(it, which):
        return pltpu.make_async_remote_copy(
            pvec.at[it, which], pvec.at[it, which], pv_send.at[it], pv_recv.at[it], mate, MESH
        )

    def row_copy(it, i, arriving):
        pz = z_peers[i]
        q = pz if arriving else z
        return pltpu.make_async_remote_copy(
            rowsend.at[it], rowall.at[it, q], rw_send.at[it, i], rw_recv.at[it, q], {"proto": pz}, MESH
        )

    loads[0].wait()
    tunit[...] = unit_rows(tf[...].astype(F32)).astype(BF16)
    lax.fori_loop(0, steps, teacher, 0)
    loads[1].wait()
    su = unit_rows(sf[...].astype(F32))
    sunit[...] = su.astype(BF16)
    turned = su.T.reshape(CHIPS, 2, 8, rows)
    for c in range(2):
        sturn[c] = turned[:, c].reshape(CHIPS * 8, rows).astype(BF16)
    smass[...] = jnp.zeros_like(smass)
    pl.semaphore_wait(barrier, 1 + len(chip_peers) + len(z_peers))

    share = ((0, 4), (4, 7), (7, 11), (11, 14), (14, 16), (16, 16))
    for it in range(ITERS):
        if it > 0:
            col_pass()
        cc = core_copy(it)
        cc.start()
        cc.wait()
        mine = colpart[core] + corecol[it]
        colsend[it] = mine
        colall[it, chip] = mine
        for i in range(len(chip_peers)):
            col_copy(it, i, False).start()
        lax.fori_loop(*share[2 * it], student, 0)
        for i in range(len(chip_peers)):
            col_copy(it, i, True).wait_recv()
        total = colall[it, 0]
        for q in range(1, CHIPS):
            total = total + colall[it, q]
        pvec[it, core] = 1.0 / (protos_all * total)
        pv_copy(it, core).start()
        pv_copy(it, 1 - core).wait_recv()
        for h in range(2):
            pscale[:, h * half : (h + 1) * half] = jnp.broadcast_to(pvec[it, h], (8, half))
        row_pass()
        rowsend[it, 0] = lane_total(rmass[...])
        rowsend[it, 1] = lane_total(smass[...]) if it == ITERS - 1 else jnp.zeros((1, rows), F32)
        rowall[it, z] = rowsend[it]
        for i in range(len(z_peers)):
            row_copy(it, i, False).start()
        lax.fori_loop(*share[2 * it + 1], student, 0)
        for i in range(len(z_peers)):
            row_copy(it, i, True).wait_recv()
        mass = rowall[it, 0]
        for q in range(1, NZ):
            mass = mass + rowall[it, q]
        if it < ITERS - 1:
            rscale[...] = down(1.0 / (crops_all * mass[0]))
        else:
            bscale[...] = down(GRAD_SCALE / mass[0])
            ascale[...] = down(GRAD_SCALE / mass[1])
        for i in range(len(chip_peers)):
            col_copy(it, i, False).wait_send()
        pv_copy(it, core).wait_send()
        for i in range(len(z_peers)):
            row_copy(it, i, False).wait_send()

    unit_acc[...] = jnp.zeros_like(unit_acc)

    def g_copy(t):
        return pltpu.make_async_remote_copy(
            gsend.at[lax.rem(t, 2)], grecv.at[t], g_send.at[lax.rem(t, 2)], g_recv.at[t], mate, MESH
        )

    def near(h, k):
        i, o = (x, y) if h == 0 else (y, x)
        p = lax.rem(i + k, 4)
        return i, p, (at(p, y, core) if h == 0 else at(x, p, core))

    def l1_copy(t, h, k, arriving):
        i, p, dev = near(h, k)
        s = lax.rem(t, 4)
        return pltpu.make_async_remote_copy(
            hold.at[s, h, p],
            land1.at[t, h, p if arriving else i],
            l1_send.at[s, h, k],
            l1_recv.at[t, h, p if arriving else i],
            dev,
            MESH,
        )

    def l2_copy(t, h, k, arriving):
        i, p, dev = near(1 - h, k)
        s = lax.rem(t, 4)
        return pltpu.make_async_remote_copy(
            hold2.at[s, h, p],
            land2.at[t, h, p if arriving else i],
            l2_send.at[s, h, k],
            l2_recv.at[t, h, p if arriving else i],
            dev,
            MESH,
        )

    def compute(t):
        cols = pl.ds(pl.multiple_of(t * W, W), W)
        for rb in range(rows // 64):
            rs = slice(rb * 64, rb * 64 + 64)
            a, b = ascale[rs, :], bscale[rs, :]
            for k in range(W // 128):
                cs = pl.ds(pl.multiple_of(t * W + k * 128, 128), 128)
                tgt = (expo[rs, cs].reshape(8, 8, 128) * pscale[:, cs][None]).reshape(64, 128)
                scores[rs, k * 128 : (k + 1) * 128] = (sexp[rs, cs] * a - tgt * b).astype(BF16)

        @pl.when(t >= 2)
        def _():
            g_copy(t).wait_send()

        gsend[lax.rem(t, 2)] = jnp.dot(sturn[1 - core], scores[...], preferred_element_type=F32)
        g_copy(t).start()
        gown[lax.rem(t, 2)] = jnp.dot(sturn[core], scores[...], preferred_element_type=F32)
        unit_acc[...] += lax.dot_general(
            scores[...], sw[:, cols], (((1,), (1,)), ((), ())), preferred_element_type=F32
        )

    def first(t):
        s = lax.rem(t, 4)
        g_copy(t).wait_recv()

        @pl.when(t >= 4)
        def _():
            for h in range(2):
                for k in range(1, 4):
                    l1_copy(t, h, k, False).wait_send()

        total = (gown[lax.rem(t, 2)] + grecv[t]).reshape(NX, NY, 8, W)
        hold[s, 0] = total[..., :hw]
        for i in range(NX):
            hold[s, 1, :, i] = total[i, ..., hw:]
        for h in range(2):
            for k in range(1, 4):
                l1_copy(t, h, k, False).start()
            i = near(h, 0)[0]
            land1[t, h, i] = hold[s, h, i]

    def second(t):
        s = lax.rem(t, 4)

        @pl.when(t >= 4)
        def _():
            for h in range(2):
                for k in range(1, 4):
                    l2_copy(t, h, k, False).wait_send()

        for h in range(2):
            for k in range(1, 4):
                l1_copy(t, h, k, True).wait_recv()
            total = land1[t, h, 0] + land1[t, h, 1] + land1[t, h, 2] + land1[t, h, 3]
            hold2[s, h] = total
            for k in range(1, 4):
                l2_copy(t, h, k, False).start()
            i = near(1 - h, 0)[0]
            land2[t, h, i] = hold2[s, h, i]

    def third(t):
        for h in range(2):
            for k in range(1, 4):
                l2_copy(t, h, k, True).wait_recv()
            total = land2[t, h, 0] + land2[t, h, 1] + land2[t, h, 2] + land2[t, h, 3]
            pout[:, pl.ds(pl.multiple_of(t * W + h * hw, hw), hw)] = total

    def u_copy(i, arriving):
        pz = z_peers[i]
        return pltpu.make_async_remote_copy(
            unit_acc.at[pl.ds(pl.multiple_of(pz * 64, 64), 64)],
            unit_in.at[pz if arriving else z],
            u_send.at[i],
            u_recv.at[pz if arriving else z],
            {"proto": pz},
            MESH,
        )

    def b_copy(i, arriving):
        pz = z_peers[i]
        return pltpu.make_async_remote_copy(
            bres, ball.at[pz if arriving else z], b_send.at[i], b_recv.at[pz if arriving else z], {"proto": pz}, MESH
        )

    def step(t, _):
        @pl.when(t < steps)
        def _():
            compute(t)

        @pl.when(t == steps)
        def _():
            for i in range(NZ - 1):
                u_copy(i, False).start()

        @pl.when((t >= 1) & (t < steps + 1))
        def _():
            first(t - 1)

        @pl.when((t >= 2) & (t < steps + 2))
        def _():
            second(t - 2)

        @pl.when((t >= 3) & (t < steps + 3))
        def _():
            third(t - 3)

        return 0

    lax.fori_loop(0, steps + 3, step, 0)

    mine = pl.ds(pl.multiple_of(z * 64, 64), 64)
    unit_in[z] = unit_acc[mine, :]
    for i in range(NZ - 1):
        u_copy(i, True).wait_recv()
    grad = unit_in[0]
    for q in range(1, NZ):
        grad = grad + unit_in[q]
    s32 = sf[mine, :].astype(F32)
    norm = jnp.sqrt(jnp.sum(s32 * s32, axis=-1, keepdims=True) + EPS)
    u32 = s32 / norm
    along = jnp.sum(u32 * grad, axis=-1, keepdims=True)
    res = (grad - u32 * along) / norm
    bres[...] = res
    for i in range(NZ - 1):
        b_copy(i, False).start()
    ball[z] = res
    for i in range(NZ - 1):
        b_copy(i, True).wait_recv()
    for q in range(NZ):
        bout[q * 64 : (q + 1) * 64, :] = ball[q]

    for i in range(NZ - 1):
        u_copy(i, False).wait_send()
        b_copy(i, False).wait_send()
    for t in range(steps - 2, steps):
        g_copy(t).wait_send()
    for t in range(steps - 4, steps):
        for h in range(2):
            for k in range(1, 4):
                l1_copy(t, h, k, False).wait_send()
                l2_copy(t, h, k, False).wait_send()


def body(teacher_feat, student_feat, teacher_protos, student_protos):
    rows, depth = teacher_feat.shape
    width = teacher_protos.shape[1]
    steps = width // W
    hw = W // 2
    crops_all = float(rows * lax.axis_size("dp"))
    protos_all = float(width * lax.axis_size("proto"))
    dma = pltpu.SemaphoreType.DMA
    vm = pltpu.VMEM
    anyspec = pl.BlockSpec(memory_space=pl.ANY)
    vspec = pl.BlockSpec(memory_space=pltpu.VMEM)
    return pl.pallas_call(
        functools.partial(kernel, crops_all, protos_all),
        out_shape=(
            jax.ShapeDtypeStruct((rows, depth), F32),
            jax.ShapeDtypeStruct((8, width), F32),
        ),
        in_specs=[anyspec] * 4,
        out_specs=(vspec, vspec),
        scratch_shapes=[
            vm((rows, depth), BF16),
            vm((rows, depth), BF16),
            vm((depth, width), BF16),
            vm((depth, width), BF16),
            vm((rows, width), F32),
            vm((rows, width), F32),
            vm((rows, depth), BF16),
            vm((rows, depth), BF16),
            vm((2, depth // 2, rows), BF16),
            vm((rows, 128), F32),
            vm((rows, 128), F32),
            vm((rows, 128), F32),
            vm((rows, 128), F32),
            vm((rows, 128), F32),
            vm((8, width), F32),
            vm((2, 1, width // 2), F32),
            vm((ITERS, 1, width // 2), F32),
            vm((ITERS, 1, width // 2), F32),
            vm((ITERS, CHIPS, 1, width // 2), F32),
            vm((ITERS, 2, 1, width // 2), F32),
            vm((ITERS, 2, 1, rows), F32),
            vm((ITERS, NZ, 2, 1, rows), F32),
            vm((rows, W), BF16),
            vm((rows, depth), F32),
            vm((2, depth // 2, W), F32),
            vm((2, depth // 2, W), F32),
            vm((steps, depth // 2, W), F32),
            vm((4, 2, 4, 4, 8, hw), F32),
            vm((steps, 2, 4, 4, 8, hw), F32),
            vm((4, 2, 4, 8, hw), F32),
            vm((steps, 2, 4, 8, hw), F32),
            vm((NZ, rows // NZ, depth), F32),
            vm((rows // NZ, depth), F32),
            vm((NZ, rows // NZ, depth), F32),
            dma((2, steps // 2)),
            dma((2,)),
            dma((ITERS,)),
            dma((ITERS,)),
            dma((ITERS, CHIPS)),
            dma((ITERS, CHIPS)),
            dma((ITERS,)),
            dma((ITERS,)),
            dma((ITERS, NZ)),
            dma((ITERS, NZ)),
            dma((2,)),
            dma((steps,)),
            dma((4, 2, 4)),
            dma((steps, 2, 4)),
            dma((4, 2, 4)),
            dma((steps, 2, 4)),
            dma((NZ,)),
            dma((NZ,)),
            dma((NZ,)),
            dma((NZ,)),
        ],
        compiler_params=pltpu.CompilerParams(
            collective_id=0, has_side_effects=True, vmem_limit_bytes=60 * 1024 * 1024
        ),
        name="sinkhorn_head",
    )(teacher_feat, student_feat, teacher_protos, student_protos)


def solution(mesh):
    placed = (P("dp", None), P("dp", None), P(None, "proto"), P(None, "proto"))
    return jax.shard_map(
        body,
        mesh=mesh,
        in_specs=placed,
        out_specs=(P("dp", None), P("dp", "proto")),
        check_vma=False,
    )
```

time: 632 us -> 158 us (0.25)
  blocking collectives: 418 us -> 0 us
  Pallas kernels: 0 us -> 152 us
  waiting for transfers between devices: 97.1 us -> 0 us
  other arithmetic: 62.2 us -> 0 us
  matrix products: 33.9 us -> 0 us
  between operations: 15.6 us -> 0.64 us
    psum x6 -> x0, blocking collectives: 418 us -> none  [the longest x3 379 us: body(): column_mass = lax.psum(jnp.sum(expo * crop_scale[:, None], axis=0), 'dp')]
    pallas_call x0 -> x1, Pallas kernels: none -> 152 us  [body(): pl.pallas_call(functools.partial(kernel, crops_all, protos_all), out_shap...]
    psum x1 -> x0, waiting for transfers between devices: 61.5 us -> none  [body(): unit_grad = lax.psum(unit_part, 'proto')]
    reduce_sum x10 -> x0, other arithmetic: 47.8 us -> none  [the longest x3 21.5 us: body(): row_part = jnp.sum(expo * proto_scale[None, :], axis=1)]
    reduce_scatter x1 -> x0, waiting for transfers between devices: 35.6 us -> none  [body(): lax.psum_scatter(crop_contract(student_unit, scores_grad), 'dp', scatter_...]
    dot_general x4 -> x0, matrix products: 33.9 us -> none  [the longest x1 11.5 us: body(): jnp.dot(teacher_unit, teacher_wunit, preferred_element_type=jnp.float32)]
    convert_element_type x1 -> x0, other arithmetic: 12.2 us -> none  [body(): scores_grad = (LOSS_SCALE / 0.1 * (probs - targets)).astype(jnp.bfloat16)]
  transfers between devices with their start and end apart: 2 -> 0, of which waited for: 2 -> 0; matrix products, arithmetic and copies ran while one was open for 2% -> 0% of each run, Pallas kernels for 0% -> 0%
where the time goes in v1:
time: 158 us; the launch traced here: 156 us
  Pallas kernels  152 us (96%)
  local copies, waits for them, and re-layouts  3.54 us (2%)
    pallas_call x1, Pallas kernels, body(): pl.pallas_call(functools.partial(kernel, crops_all, protos_all), out_shap...  152 us
    unnamed x2, local copies, waits for them, and re-layouts  3.54 us

profile of v1, /device:TPU:1, one launch (start us, length us, event | category | flops | bytes accessed | tf_op | source)
XLA Modules:
  0.0 156.2 jit_solution(1049506283443932193)
XLA Ops:
  0.6 152.0 %sinkhorn_head.1 = (f32[512,256]{1,0:T(8,128)}, f32[8,8192]{1,0:T(8,128)}) custom-call(bf16[512,256]{1,0:T(8,128)(2,1)} %tf_hbm.1, bf16[512,256]{1,0:T(8,128)(2,1)} %sf_hbm.1, bf16[256,8192]{1,0:T(8,128)(2,1)} %tw_hbm.1, bf16[256,8192]{1,0:T(8,128)(2,1)} %sw_hbm.1), custom_call_target="tpu_custom_call" | custom-call | tf_op jit(solution)/shard_map/sinkhorn_head/pallas_call | solution.py:493
  152.6 1.9 %copy.8 = f32[512,256]{1,0:T(8,128)} copy(f32[512,256]{1,0:T(8,128)} %get-tuple-element.4) | data formatting | bytes 1048576
  154.5 1.7 %copy.9 = f32[8,8192]{1,0:T(8,128)} copy(f32[8,8192]{1,0:T(8,128)} %get-tuple-element.5) | data formatting | bytes 524288

commit v2 on v1

v2 whole, which is shorter than its diff:
```python
import functools
import math

import jax
import jax.numpy as jnp
from jax import lax
from jax.experimental import pallas as pl
from jax.experimental.pallas import tpu as pltpu
from jax.sharding import PartitionSpec as P

F32 = jnp.float32
BF16 = jnp.bfloat16
MESH = pl.DeviceIdType.MESH
ITERS = 3
GRAD_SCALE = 256 / 0.1
TEACHER_RATE = math.log2(math.e) / 0.05
STUDENT_RATE = math.log2(math.e) / 0.1
EPS = 1e-06
TINY = 1.2e-38
NX, NY, NZ = 4, 4, 8
CHIPS = NX * NY
W = 1024
WIDE = 2048
BLOCK = 512
FINE = 256


def encode(v, power):
    square = v * v
    fourth = square * square
    return (fourth * v if power == 5 else fourth * square * v).astype(BF16)


def decode(code, power):
    c = code.astype(F32)
    size = jnp.exp2(jnp.log2(jnp.maximum(jnp.abs(c), TINY)) * (1.0 / power))
    return jnp.where(c < 0, -size, size)


def unit_rows(x):
    return x / jnp.sqrt(jnp.sum(x * x, axis=-1, keepdims=True) + EPS)


def kernel(
    crops_all,
    protos_all,
    tf_hbm,
    sf_hbm,
    tw_hbm,
    sw_hbm,
    bout,
    pout,
    tf,
    sf,
    tw,
    swt,
    expo,
    sexp,
    tunit,
    sunit,
    sturn,
    smass,
    rmass,
    rscale,
    ascale,
    bscale,
    pscale,
    colpart,
    corecol,
    colsend,
    colall,
    pvec,
    rowsend,
    rowall,
    unit_acc,
    gsend,
    gown,
    grecv,
    swap,
    land1,
    hold2,
    kept2,
    land2,
    unit_out,
    unit_in,
    bres,
    ball,
    load_sem,
    feat_sem,
    cc_send,
    cc_recv,
    ca_send,
    ca_recv,
    pv_send,
    pv_recv,
    rw_send,
    rw_recv,
    g_send,
    g_recv,
    l1_send,
    l1_recv,
    l2_send,
    l2_recv,
    u_send,
    u_recv,
    b_send,
    b_recv,
):
    rows, depth = tf.shape
    width = tw.shape[1]
    half = width // 2
    steps = width // W
    hw = W // 2
    d = lax.axis_index("dp")
    z = lax.axis_index("proto")
    core = lax.rem(d, 2)
    chip = lax.div(d, 2)
    x = lax.div(chip, NY)
    y = lax.rem(chip, NY)

    def at(px, py, pc):
        return {"dp": (px * NY + py) * 2 + pc}

    mate = at(x, y, 1 - core)
    chip_peers = []
    for k in range(1, CHIPS):
        px, py = lax.rem(x + k // NY, NX), lax.rem(y + k % NY, NY)
        chip_peers.append((px * NY + py, at(px, py, core)))
    z_peers = [lax.rem(z + k, NZ) for k in range(1, NZ)]

    loads = []
    for i, (src, dst) in enumerate(((tf_hbm, tf), (sf_hbm, sf))):
        c = pltpu.make_async_copy(src, dst, feat_sem.at[i])
        c.start()
        loads.append(c)

    def load(which, src, t):
        cols = pl.ds(pl.multiple_of(t * W, W), W)
        return pltpu.make_async_copy(src.at[:, cols], tw.at[:, cols], load_sem.at[which, t])

    for t in range(steps):
        load(0, tw_hbm, t).start()

    barrier = pltpu.get_barrier_semaphore()
    pl.semaphore_signal(barrier, inc=1, device_id=mate, device_id_type=MESH)
    for _, dev in chip_peers:
        pl.semaphore_signal(barrier, inc=1, device_id=dev, device_id_type=MESH)
    for pz in z_peers:
        pl.semaphore_signal(barrier, inc=1, device_id={"proto": pz}, device_id_type=MESH)

    def unit_block(cols):
        w32 = tw[:, cols].astype(F32)
        inv = 1.0 / jnp.sqrt(jnp.sum(w32 * w32, axis=0, keepdims=True) + EPS)
        return (w32 * inv).astype(BF16)

    def teacher(t, _):
        for i in range(WIDE // W):
            load(0, tw_hbm, t * (WIDE // W) + i).wait()
        for o in range(0, WIDE, BLOCK):
            cols = pl.ds(pl.multiple_of(t * WIDE + o, BLOCK), BLOCK)
            e = jnp.exp2(jnp.dot(tunit[...], unit_block(cols), preferred_element_type=F32) * TEACHER_RATE)
            expo[:, cols] = e
            off = pl.ds(pl.multiple_of(lax.rem(t, 2) * WIDE + o, BLOCK), BLOCK)
            colpart[lax.div(t, 2), :, off] = jnp.sum(e, axis=0, keepdims=True)
        return 0

    def student(t, _):
        for i in range(WIDE // W):
            load(1, sw_hbm, t * (WIDE // W) + i).wait()
        acc = smass[...]
        for o in range(0, WIDE, BLOCK):
            cols = pl.ds(pl.multiple_of(t * WIDE + o, BLOCK), BLOCK)
            w = unit_block(cols)
            swt[cols, :] = w.T
            e = jnp.exp2(jnp.dot(sunit[...], w, preferred_element_type=F32) * STUDENT_RATE)
            sexp[:, cols] = e
            for k in range(BLOCK // 128):
                acc = acc + e[:, k * 128 : (k + 1) * 128]
        smass[...] = acc
        return 0

    def row_pass():
        def block(i, _):
            rs = pl.ds(pl.multiple_of(i * 128, 128), 128)
            acc = [jnp.zeros((16, 8, 128), F32)] * 2
            for k in range(width // 128):
                cs = slice(k * 128, (k + 1) * 128)
                acc[k % 2] = acc[k % 2] + expo[rs, cs].reshape(16, 8, 128) * pscale[:, cs][None]
            rmass[rs, :] = (acc[0] + acc[1]).reshape(128, 128)
            return 0

        lax.fori_loop(0, rows // 128, block, 0)

    def col_pass():
        def block(j, _):
            cs = pl.ds(pl.multiple_of(j * 1024, 1024), 1024)
            acc = [jnp.zeros((8, 1024), F32)] * 2
            for i in range(rows // 8):
                r = rscale[i * 8 : i * 8 + 8, :]
                acc[i % 2] = acc[i % 2] + expo[i * 8 : i * 8 + 8, cs] * jnp.concatenate([r] * 8, axis=1)
            off = pl.ds(pl.multiple_of(lax.rem(j, 4) * 1024, 1024), 1024)
            colpart[lax.div(j, 4), :, off] = jnp.sum(acc[0] + acc[1], axis=0, keepdims=True)
            return 0

        lax.fori_loop(0, width // 1024, block, 0)

    def lane_total(acc):
        return jnp.sum(acc.T, axis=0, keepdims=True)

    def down(vec):
        return jnp.broadcast_to(vec, (128, rows)).T

    def core_copy(it):
        return pltpu.make_async_remote_copy(
            colpart.at[1 - core], corecol.at[it], cc_send.at[it], cc_recv.at[it], mate, MESH
        )

    def col_copy(it, i, arriving):
        q, dev = chip_peers[i]
        q = q if arriving else chip
        return pltpu.make_async_remote_copy(
            colsend.at[it], colall.at[it, q], ca_send.at[it, i], ca_recv.at[it, q], dev, MESH
        )

    def pv_copy(it, which):
        return pltpu.make_async_remote_copy(
            pvec.at[it, which], pvec.at[it, which], pv_send.at[it], pv_recv.at[it], mate, MESH
        )

    def row_copy(it, i, arriving):
        pz = z_peers[i]
        q = pz if arriving else z
        return pltpu.make_async_remote_copy(
            rowsend.at[it], rowall.at[it, q], rw_send.at[it, i], rw_recv.at[it, q], {"proto": pz}, MESH
        )

    loads[0].wait()
    tunit[...] = unit_rows(tf[...].astype(F32)).astype(BF16)
    lax.fori_loop(0, width // WIDE, teacher, 0)
    for t in range(steps):
        load(1, sw_hbm, t).start()
    loads[1].wait()
    su = unit_rows(sf[...].astype(F32))
    sunit[...] = su.astype(BF16)
    turned = su.T.reshape(CHIPS, 2, 8, rows)
    for c in range(2):
        sturn[c * core + (1 - c) * (1 - core)] = turned[:, c].reshape(CHIPS * 8, rows).astype(BF16)
    smass[...] = jnp.zeros_like(smass)
    pl.semaphore_wait(barrier, 1 + len(chip_peers) + len(z_peers))

    share = ((0, 1), (1, 2), (2, 3), (3, 4), (4, 4), (4, 4))
    for it in range(ITERS):
        if it > 0:
            col_pass()
        cc = core_copy(it)
        cc.start()
        cc.wait()
        mine = colpart[core] + corecol[it]
        colsend[it] = mine
        colall[it, chip] = mine
        for i in range(len(chip_peers)):
            col_copy(it, i, False).start()
        lax.fori_loop(*share[2 * it], student, 0)
        for i in range(len(chip_peers)):
            col_copy(it, i, True).wait_recv()
        total = colall[it, 0]
        for q in range(1, CHIPS):
            total = total + colall[it, q]
        pvec[it, core] = 1.0 / (protos_all * total)
        pv_copy(it, core).start()
        pv_copy(it, 1 - core).wait_recv()
        for h in range(2):
            pscale[:, h * half : (h + 1) * half] = jnp.broadcast_to(pvec[it, h], (8, half))
        row_pass()
        rowsend[it, 0] = lane_total(rmass[...])
        rowsend[it, 1] = lane_total(smass[...]) if it == ITERS - 1 else jnp.zeros((1, rows), F32)
        rowall[it, z] = rowsend[it]
        for i in range(len(z_peers)):
            row_copy(it, i, False).start()
        lax.fori_loop(*share[2 * it + 1], student, 0)
        for i in range(len(z_peers)):
            row_copy(it, i, True).wait_recv()
        mass = rowall[it, 0]
        for q in range(1, NZ):
            mass = mass + rowall[it, q]
        if it < ITERS - 1:
            rscale[...] = down(1.0 / (crops_all * mass[0]))
        else:
            bscale[...] = down(GRAD_SCALE / mass[0])
            ascale[...] = down(GRAD_SCALE / mass[1])
        for i in range(len(chip_peers)):
            col_copy(it, i, False).wait_send()
        pv_copy(it, core).wait_send()
        for i in range(len(z_peers)):
            row_copy(it, i, False).wait_send()

    unit_acc[...] = jnp.zeros_like(unit_acc)

    def g_copy(t):
        s = lax.rem(t, 3)
        return pltpu.make_async_remote_copy(gsend.at[s], grecv.at[t], g_send.at[s], g_recv.at[t], mate, MESH)

    def near(h, k):
        i, o = (x, y) if h == 0 else (y, x)
        p = lax.rem(i + k, 4)
        return i, p, (at(p, y, core) if h == 0 else at(x, p, core))

    def hold(t, h, p):
        return pl.ds(pl.multiple_of((h * 4 + p) * 32, 32), 32), pl.ds(pl.multiple_of(t * hw, hw), hw)

    def l1_copy(t, h, k, arriving):
        i, p, dev = near(h, k)
        q = p if arriving else i
        return pltpu.make_async_remote_copy(
            tw.at[hold(t, h, p)], land1.at[t, h, q], l1_send.at[t, h, k], l1_recv.at[t, h, q], dev, MESH
        )

    def l2_copy(t, h, k, arriving):
        i, p, dev = near(1 - h, k)
        q = p if arriving else i
        return pltpu.make_async_remote_copy(
            hold2.at[t, h, p], land2.at[t, h, q], l2_send.at[t, h, k], l2_recv.at[t, h, q], dev, MESH
        )

    def compute(t):
        turn = sturn[...].reshape(depth, rows)
        slot = lax.rem(t, 3)
        unit = None

        @pl.when(t >= 3)
        def _():
            g_copy(t).wait_send()

        for o in range(0, W, FINE):
            blocks = []
            for rb in range(rows // 64):
                rs = slice(rb * 64, rb * 64 + 64)
                line = []
                for k in range(FINE // 128):
                    cs = pl.ds(pl.multiple_of(t * W + o + k * 128, 128), 128)
                    tgt = (expo[rs, cs].reshape(8, 8, 128) * pscale[:, cs][None]).reshape(64, 128)
                    line.append((sexp[rs, cs] * ascale[rs, :] - tgt * bscale[rs, :]).astype(BF16))
                blocks.append(jnp.concatenate(line, axis=1))
            score = jnp.concatenate(blocks, axis=0)
            g = jnp.dot(turn, score, preferred_element_type=F32)
            gsend[slot, :, o : o + FINE] = g[: depth // 2]
            gown[slot, :, o : o + FINE] = g[depth // 2 :]
            cols = pl.ds(pl.multiple_of(t * W + o, FINE), FINE)
            part = jnp.dot(score, swt[cols, :], preferred_element_type=F32)
            unit = part if unit is None else unit + part
        unit_acc[...] += unit
        g_copy(t).start()

    def first(t):
        g_copy(t).wait_recv()
        for i in range(NX):
            part = (gown[lax.rem(t, 3), i * 32 : i * 32 + 32] + grecv[t, i * 32 : i * 32 + 32]).reshape(NY, 8, W)
            grecv[t, i * 32 : i * 32 + 32] = part.reshape(NY * 8, W)
            code = encode(part, 5)
            tw[hold(t, 0, i)] = code[..., :hw].reshape(NY * 8, hw)
            for j in range(NY):
                swap[i, j] = part[j, :, hw:]
        for j in range(NY):
            tw[hold(t, 1, j)] = encode(swap[:, j], 5).reshape(NX * 8, hw)
        for h in range(2):
            for k in range(1, 4):
                l1_copy(t, h, k, False).start()

    def second(t):
        for h in range(2):
            if h == 0:
                total = grecv[t, pl.ds(pl.multiple_of(x * 32, 32), 32), :hw].reshape(4, 8, hw)
            else:
                total = jnp.stack(
                    [grecv[t, pl.ds(pl.multiple_of(i * 32 + y * 8, 8), 8), hw:] for i in range(NX)], axis=0
                )
            for k in range(1, 4):
                l1_copy(t, h, k, True).wait_recv()
                total = total + decode(land1[t, h, near(h, k)[1]], 5).reshape(4, 8, hw)
            kept2[t, h] = total
            for i in range(4):
                v = total[i]
                hold2[t, h, i] = encode(jnp.concatenate([v[:, : hw // 2], v[:, hw // 2 :]], axis=0), 5)
            for k in range(1, 4):
                l2_copy(t, h, k, False).start()

    def third(t):
        for h in range(2):
            total = kept2[t, h, near(1 - h, 0)[0]]
            for k in range(1, 4):
                l2_copy(t, h, k, True).wait_recv()
                v = decode(land2[t, h, near(1 - h, k)[1]], 5)
                total = total + jnp.concatenate([v[:8], v[8:]], axis=1)
            pout[:, pl.ds(pl.multiple_of(t * W + h * hw, hw), hw)] = total

    def u_copy(i, arriving):
        pz = z_peers[i]
        return pltpu.make_async_remote_copy(
            unit_out.at[pz],
            unit_in.at[pz if arriving else z],
            u_send.at[i],
            u_recv.at[pz if arriving else z],
            {"proto": pz},
            MESH,
        )

    def b_copy(i, arriving):
        pz = z_peers[i]
        return pltpu.make_async_remote_copy(
            bres, ball.at[pz if arriving else z], b_send.at[i], b_recv.at[pz if arriving else z], {"proto": pz}, MESH
        )

    def step(t, _):
        compute(t)

        @pl.when(t >= 2)
        def _():
            first(t - 2)

        @pl.when(t >= 5)
        def _():
            second(t - 5)

        return 0

    def run(lo, hi, fn):
        def one(t, _):
            fn(t)
            return 0

        lax.fori_loop(lo, hi, one, 0)

    lax.fori_loop(0, steps, step, 0)
    unit_out[...] = encode(unit_acc[...], 7).reshape(NZ, rows // NZ, depth)
    for i in range(NZ - 1):
        u_copy(i, False).start()
    run(steps - 2, steps, first)
    run(steps - 5, steps - 2, second)
    run(0, 3, third)

    mine = pl.ds(pl.multiple_of(z * 64, 64), 64)
    grad = unit_acc[mine, :]
    for i in range(NZ - 1):
        u_copy(i, True).wait_recv()
        grad = grad + decode(unit_in[z_peers[i]], 7)
    u32 = unit_rows(sf[mine, :].astype(F32))
    bres[...] = encode(grad - u32 * jnp.sum(u32 * grad, axis=-1, keepdims=True), 7)
    for i in range(NZ - 1):
        b_copy(i, False).start()
    ball[z] = bres[...]

    run(steps - 2, steps, second)
    run(3, steps, third)

    for i in range(NZ - 1):
        b_copy(i, True).wait_recv()
    for q in range(NZ):
        rs = slice(q * 64, q * 64 + 64)
        s32 = sf[rs, :].astype(F32)
        norm = jnp.sqrt(jnp.sum(s32 * s32, axis=-1, keepdims=True) + EPS)
        bout[rs, :] = decode(ball[q], 7) / norm

    for i in range(NZ - 1):
        u_copy(i, False).wait_send()
        b_copy(i, False).wait_send()
    for t in range(steps - 3, steps):
        g_copy(t).wait_send()

    def drain(t):
        for h in range(2):
            for k in range(1, 4):
                l1_copy(t, h, k, False).wait_send()
                l2_copy(t, h, k, False).wait_send()

    run(0, steps, drain)


def body(teacher_feat, student_feat, teacher_protos, student_protos):
    rows, depth = teacher_feat.shape
    width = teacher_protos.shape[1]
    steps = width // W
    hw = W // 2
    crops_all = float(rows * lax.axis_size("dp"))
    protos_all = float(width * lax.axis_size("proto"))
    dma = pltpu.SemaphoreType.DMA
    vm = pltpu.VMEM
    anyspec = pl.BlockSpec(memory_space=pl.ANY)
    vspec = pl.BlockSpec(memory_space=pltpu.VMEM)
    return pl.pallas_call(
        functools.partial(kernel, crops_all, protos_all),
        out_shape=(
            jax.ShapeDtypeStruct((rows, depth), F32),
            jax.ShapeDtypeStruct((8, width), F32),
        ),
        in_specs=[anyspec] * 4,
        out_specs=(vspec, vspec),
        scratch_shapes=[
            vm((rows, depth), BF16),
            vm((rows, depth), BF16),
            vm((depth, width), BF16),
            vm((width, depth), BF16),
            vm((rows, width), F32),
            vm((rows, width), F32),
            vm((rows, depth), BF16),
            vm((rows, depth), BF16),
            vm((2, depth // 2, rows), BF16),
            vm((rows, 128), F32),
            vm((rows, 128), F32),
            vm((rows, 128), F32),
            vm((rows, 128), F32),
            vm((rows, 128), F32),
            vm((8, width), F32),
            vm((2, 1, width // 2), F32),
            vm((ITERS, 1, width // 2), F32),
            vm((ITERS, 1, width // 2), F32),
            vm((ITERS, CHIPS, 1, width // 2), F32),
            vm((ITERS, 2, 1, width // 2), F32),
            vm((ITERS, 2, 1, rows), F32),
            vm((ITERS, NZ, 2, 1, rows), F32),
            vm((rows, depth), F32),
            vm((3, depth // 2, W), F32),
            vm((3, depth // 2, W), F32),
            vm((steps, depth // 2, W), F32),
            vm((NX, NY, 8, hw), F32),
            vm((steps, 2, 4, 32, hw), BF16),
            vm((steps, 2, 4, 16, hw // 2), BF16),
            vm((steps, 2, 4, 8, hw), F32),
            vm((steps, 2, 4, 16, hw // 2), BF16),
            vm((NZ, rows // NZ, depth), BF16),
            vm((NZ, rows // NZ, depth), BF16),
            vm((rows // NZ, depth), BF16),
            vm((NZ, rows // NZ, depth), BF16),
            dma((2, steps)),
            dma((2,)),
            dma((ITERS,)),
            dma((ITERS,)),
            dma((ITERS, CHIPS)),
            dma((ITERS, CHIPS)),
            dma((ITERS,)),
            dma((ITERS,)),
            dma((ITERS, NZ)),
            dma((ITERS, NZ)),
            dma((3,)),
            dma((steps,)),
            dma((steps, 2, 4)),
            dma((steps, 2, 4)),
            dma((steps, 2, 4)),
            dma((steps, 2, 4)),
            dma((NZ,)),
            dma((NZ,)),
            dma((NZ,)),
            dma((NZ,)),
        ],
        compiler_params=pltpu.CompilerParams(
            collective_id=0, has_side_effects=True, vmem_limit_bytes=62 * 1024 * 1024
        ),
        name="sinkhorn_head",
    )(teacher_feat, student_feat, teacher_protos, student_protos)


def solution(mesh):
    placed = (P("dp", None), P("dp", None), P(None, "proto"), P(None, "proto"))
    return jax.shard_map(
        body,
        mesh=mesh,
        in_specs=placed,
        out_specs=(P("dp", None), P("dp", "proto")),
        check_vma=False,
    )
```

time: 158 us -> 95.7 us (0.61); the launches traced: 156 us -> 95.6 us
  Pallas kernels: 152 us -> 91.4 us
    pallas_call x1, Pallas kernels: 152 us -> 91.4 us  [body(): pl.pallas_call(functools.partial(kernel, crops_all, protos_all), out_shap...]
where the time goes in v2:
time: 95.7 us; the launch traced here: 95.6 us
  Pallas kernels  91.4 us (96%)
  local copies, waits for them, and re-layouts  3.54 us (4%)
    pallas_call x1, Pallas kernels, body(): pl.pallas_call(functools.partial(kernel, crops_all, protos_all), out_shap...  91.4 us
    unnamed x2, local copies, waits for them, and re-layouts  3.54 us

profile of v2, /device:TPU:1, one launch (start us, length us, event | category | flops | bytes accessed | tf_op | source)
XLA Modules:
  0.0 95.6 jit_solution(1008145048918428707)
XLA Ops:
  0.6 91.4 %sinkhorn_head.1 = (f32[512,256]{1,0:T(8,128)}, f32[8,8192]{1,0:T(8,128)}) custom-call(bf16[512,256]{1,0:T(8,128)(2,1)} %tf_hbm.1, bf16[512,256]{1,0:T(8,128)(2,1)} %sf_hbm.1, bf16[256,8192]{1,0:T(8,128)(2,1)} %tw_hbm.1, bf16[256,8192]{1,0:T(8,128)(2,1)} %sw_hbm.1), custom_call_target="tpu_custom_call" | custom-call | tf_op jit(solution)/shard_map/sinkhorn_head/pallas_call | solution.py:489
  92.0 1.9 %copy.8 = f32[512,256]{1,0:T(8,128)} copy(f32[512,256]{1,0:T(8,128)} %get-tuple-element.4) | data formatting | bytes 1048576
  93.9 1.7 %copy.9 = f32[8,8192]{1,0:T(8,128)} copy(f32[8,8192]{1,0:T(8,128)} %get-tuple-element.5) | data formatting | bytes 524288

commit v3 on v2

--- a/solution.py
+++ b/solution.py
@@ -23,6 +23,7 @@
 WIDE = 2048
 BLOCK = 512
 FINE = 256
+PART = 32
 
 
 def encode(v, power):
@@ -126,7 +127,7 @@
     for k in range(1, CHIPS):
         px, py = lax.rem(x + k // NY, NX), lax.rem(y + k % NY, NY)
         chip_peers.append((px * NY + py, at(px, py, core)))
-    z_peers = [lax.rem(z + k, NZ) for k in range(1, NZ)]
+    z_peers = [lax.rem(z + k, NZ) for k in (4, 3, 5, 2, 6, 1, 7)]
 
     loads = []
     for i, (src, dst) in enumerate(((tf_hbm, tf), (sf_hbm, sf))):
@@ -134,9 +135,14 @@
         c.start()
         loads.append(c)
 
+    def place(t):
+        h = t // (steps // 2)
+        return (h * core + (1 - h) * (1 - core)) * (steps // 2) + t % (steps // 2)
+
     def load(which, src, t):
         cols = pl.ds(pl.multiple_of(t * W, W), W)
-        return pltpu.make_async_copy(src.at[:, cols], tw.at[:, cols], load_sem.at[which, t])
+        mine = pl.ds(pl.multiple_of(place(t) * W, W), W)
+        return pltpu.make_async_copy(src.at[:, mine], tw.at[:, cols], load_sem.at[which, t])
 
     for t in range(steps):
         load(0, tw_hbm, t).start()
@@ -179,30 +185,34 @@
         smass[...] = acc
         return 0
 
-    def row_pass():
+    def row_pass(h, fresh):
         def block(i, _):
             rs = pl.ds(pl.multiple_of(i * 128, 128), 128)
-            acc = [jnp.zeros((16, 8, 128), F32)] * 2
-            for k in range(width // 128):
-                cs = slice(k * 128, (k + 1) * 128)
+            zero = jnp.zeros((16, 8, 128), F32)
+            acc = [zero if fresh else rmass[rs, :].reshape(16, 8, 128), zero]
+            for k in range(half // 128):
+                cs = slice(h * half + k * 128, h * half + k * 128 + 128)
                 acc[k % 2] = acc[k % 2] + expo[rs, cs].reshape(16, 8, 128) * pscale[:, cs][None]
             rmass[rs, :] = (acc[0] + acc[1]).reshape(128, 128)
             return 0
 
         lax.fori_loop(0, rows // 128, block, 0)
 
-    def col_pass():
+    def col_pass(h):
         def block(j, _):
-            cs = pl.ds(pl.multiple_of(j * 1024, 1024), 1024)
+            cs = pl.ds(pl.multiple_of(h * half + j * 1024, 1024), 1024)
             acc = [jnp.zeros((8, 1024), F32)] * 2
             for i in range(rows // 8):
                 r = rscale[i * 8 : i * 8 + 8, :]
                 acc[i % 2] = acc[i % 2] + expo[i * 8 : i * 8 + 8, cs] * jnp.concatenate([r] * 8, axis=1)
-            off = pl.ds(pl.multiple_of(lax.rem(j, 4) * 1024, 1024), 1024)
-            colpart[lax.div(j, 4), :, off] = jnp.sum(acc[0] + acc[1], axis=0, keepdims=True)
+            off = pl.ds(pl.multiple_of(j * 1024, 1024), 1024)
+            colpart[h, :, off] = jnp.sum(acc[0] + acc[1], axis=0, keepdims=True)
             return 0
 
-        lax.fori_loop(0, width // 1024, block, 0)
+        lax.fori_loop(0, half // 1024, block, 0)
+
+    def spread(it, h):
+        pscale[:, h * half : (h + 1) * half] = jnp.broadcast_to(pvec[it, h], (8, half))
 
     def lane_total(acc):
         return jnp.sum(acc.T, axis=0, keepdims=True)
@@ -212,7 +222,7 @@
 
     def core_copy(it):
         return pltpu.make_async_remote_copy(
-            colpart.at[1 - core], corecol.at[it], cc_send.at[it], cc_recv.at[it], mate, MESH
+            colpart.at[0], corecol.at[it], cc_send.at[it], cc_recv.at[it], mate, MESH
         )
 
     def col_copy(it, i, arriving):
@@ -222,9 +232,9 @@
             colsend.at[it], colall.at[it, q], ca_send.at[it, i], ca_recv.at[it, q], dev, MESH
         )
 
-    def pv_copy(it, which):
-        return pltpu.make_async_remote_copy(
-            pvec.at[it, which], pvec.at[it, which], pv_send.at[it], pv_recv.at[it], mate, MESH
+    def pv_copy(it):
+        return pltpu.make_async_remote_copy(
+            pvec.at[it, 1], pvec.at[it, 0], pv_send.at[it], pv_recv.at[it], mate, MESH
         )
 
     def row_copy(it, i, arriving):
@@ -239,39 +249,43 @@
     lax.fori_loop(0, width // WIDE, teacher, 0)
     for t in range(steps):
         load(1, sw_hbm, t).start()
-    loads[1].wait()
-    su = unit_rows(sf[...].astype(F32))
-    sunit[...] = su.astype(BF16)
-    turned = su.T.reshape(CHIPS, 2, 8, rows)
-    for c in range(2):
-        sturn[c * core + (1 - c) * (1 - core)] = turned[:, c].reshape(CHIPS * 8, rows).astype(BF16)
-    smass[...] = jnp.zeros_like(smass)
     pl.semaphore_wait(barrier, 1 + len(chip_peers) + len(z_peers))
 
     share = ((0, 1), (1, 2), (2, 3), (3, 4), (4, 4), (4, 4))
     for it in range(ITERS):
         if it > 0:
-            col_pass()
+            col_pass(0)
         cc = core_copy(it)
         cc.start()
+        if it > 0:
+            col_pass(1)
         cc.wait()
-        mine = colpart[core] + corecol[it]
+        mine = colpart[1] + corecol[it]
         colsend[it] = mine
         colall[it, chip] = mine
         for i in range(len(chip_peers)):
             col_copy(it, i, False).start()
+        if it == 0:
+            loads[1].wait()
+            su = unit_rows(sf[...].astype(F32))
+            sunit[...] = su.astype(BF16)
+            turned = su.T.reshape(CHIPS, 2, 8, rows)
+            for c in range(2):
+                sturn[c * core + (1 - c) * (1 - core)] = turned[:, c].reshape(CHIPS * 8, rows).astype(BF16)
+            smass[...] = jnp.zeros_like(smass)
         lax.fori_loop(*share[2 * it], student, 0)
         for i in range(len(chip_peers)):
             col_copy(it, i, True).wait_recv()
         total = colall[it, 0]
         for q in range(1, CHIPS):
             total = total + colall[it, q]
-        pvec[it, core] = 1.0 / (protos_all * total)
-        pv_copy(it, core).start()
-        pv_copy(it, 1 - core).wait_recv()
-        for h in range(2):
-            pscale[:, h * half : (h + 1) * half] = jnp.broadcast_to(pvec[it, h], (8, half))
-        row_pass()
+        pvec[it, 1] = 1.0 / (protos_all * total)
+        pv_copy(it).start()
+        spread(it, 1)
+        row_pass(1, True)
+        pv_copy(it).wait_recv()
+        spread(it, 0)
+        row_pass(0, False)
         rowsend[it, 0] = lane_total(rmass[...])
         rowsend[it, 1] = lane_total(smass[...]) if it == ITERS - 1 else jnp.zeros((1, rows), F32)
         rowall[it, z] = rowsend[it]
@@ -290,7 +304,7 @@
             ascale[...] = down(GRAD_SCALE / mass[1])
         for i in range(len(chip_peers)):
             col_copy(it, i, False).wait_send()
-        pv_copy(it, core).wait_send()
+        pv_copy(it).wait_send()
         for i in range(len(z_peers)):
             row_copy(it, i, False).wait_send()
 
@@ -326,6 +340,7 @@
         turn = sturn[...].reshape(depth, rows)
         slot = lax.rem(t, 3)
         unit = None
+        here = place(t)
 
         @pl.when(t >= 3)
         def _():
@@ -337,7 +352,7 @@
                 rs = slice(rb * 64, rb * 64 + 64)
                 line = []
                 for k in range(FINE // 128):
-                    cs = pl.ds(pl.multiple_of(t * W + o + k * 128, 128), 128)
+                    cs = pl.ds(pl.multiple_of(here * W + o + k * 128, 128), 128)
                     tgt = (expo[rs, cs].reshape(8, 8, 128) * pscale[:, cs][None]).reshape(64, 128)
                     line.append((sexp[rs, cs] * ascale[rs, :] - tgt * bscale[rs, :]).astype(BF16))
                 blocks.append(jnp.concatenate(line, axis=1))
@@ -345,7 +360,7 @@
             g = jnp.dot(turn, score, preferred_element_type=F32)
             gsend[slot, :, o : o + FINE] = g[: depth // 2]
             gown[slot, :, o : o + FINE] = g[depth // 2 :]
-            cols = pl.ds(pl.multiple_of(t * W + o, FINE), FINE)
+            cols = pl.ds(pl.multiple_of(here * W + o, FINE), FINE)
             part = jnp.dot(score, swt[cols, :], preferred_element_type=F32)
             unit = part if unit is None else unit + part
         unit_acc[...] += unit
@@ -393,22 +408,34 @@
                 total = total + jnp.concatenate([v[:8], v[8:]], axis=1)
             pout[:, pl.ds(pl.multiple_of(t * W + h * hw, hw), hw)] = total
 
-    def u_copy(i, arriving):
+    def u_copy(i, part, arriving):
         pz = z_peers[i]
-        return pltpu.make_async_remote_copy(
-            unit_out.at[pz],
-            unit_in.at[pz if arriving else z],
-            u_send.at[i],
-            u_recv.at[pz if arriving else z],
-            {"proto": pz},
-            MESH,
-        )
-
-    def b_copy(i, arriving):
+        q = pz if arriving else z
+        rs = pl.ds(part * PART, PART)
+        return pltpu.make_async_remote_copy(
+            unit_out.at[pz, rs], unit_in.at[q, rs], u_send.at[part, i], u_recv.at[part, q], {"proto": pz}, MESH
+        )
+
+    def b_copy(i, part, arriving):
         pz = z_peers[i]
-        return pltpu.make_async_remote_copy(
-            bres, ball.at[pz if arriving else z], b_send.at[i], b_recv.at[pz if arriving else z], {"proto": pz}, MESH
-        )
+        q = pz if arriving else z
+        rs = pl.ds(part * PART, PART)
+        return pltpu.make_async_remote_copy(
+            bres.at[rs], ball.at[q, rs], b_send.at[part, i], b_recv.at[part, q], {"proto": pz}, MESH
+        )
+
+    def project(part):
+        rs = pl.ds(pl.multiple_of(z * 64 + part * PART, PART), PART)
+        own = slice(part * PART, (part + 1) * PART)
+        grad = unit_acc[rs, :]
+        for i in range(NZ - 1):
+            u_copy(i, part, True).wait_recv()
+            grad = grad + decode(unit_in[z_peers[i], own], 7)
+        u32 = unit_rows(sf[rs, :].astype(F32))
+        bres[own] = encode(grad - u32 * jnp.sum(u32 * grad, axis=-1, keepdims=True), 7)
+        for i in range(NZ - 1):
+            b_copy(i, part, False).start()
+        ball[z, own] = bres[own]
 
     def step(t, _):
         compute(t)
@@ -416,10 +443,6 @@
         @pl.when(t >= 2)
         def _():
             first(t - 2)
-
-        @pl.when(t >= 5)
-        def _():
-            second(t - 5)
 
         return 0
 
@@ -432,37 +455,26 @@
 
     lax.fori_loop(0, steps, step, 0)
     unit_out[...] = encode(unit_acc[...], 7).reshape(NZ, rows // NZ, depth)
-    for i in range(NZ - 1):
-        u_copy(i, False).start()
+    for part in range(2):
+        for i in range(NZ - 1):
+            u_copy(i, part, False).start()
     run(steps - 2, steps, first)
-    run(steps - 5, steps - 2, second)
-    run(0, 3, third)
-
-    mine = pl.ds(pl.multiple_of(z * 64, 64), 64)
-    grad = unit_acc[mine, :]
-    for i in range(NZ - 1):
-        u_copy(i, True).wait_recv()
-        grad = grad + decode(unit_in[z_peers[i]], 7)
-    u32 = unit_rows(sf[mine, :].astype(F32))
-    bres[...] = encode(grad - u32 * jnp.sum(u32 * grad, axis=-1, keepdims=True), 7)
-    for i in range(NZ - 1):
-        b_copy(i, False).start()
-    ball[z] = bres[...]
-
-    run(steps - 2, steps, second)
-    run(3, steps, third)
-
-    for i in range(NZ - 1):
-        b_copy(i, True).wait_recv()
-    for q in range(NZ):
-        rs = slice(q * 64, q * 64 + 64)
-        s32 = sf[rs, :].astype(F32)
-        norm = jnp.sqrt(jnp.sum(s32 * s32, axis=-1, keepdims=True) + EPS)
-        bout[rs, :] = decode(ball[q], 7) / norm
-
-    for i in range(NZ - 1):
-        u_copy(i, False).wait_send()
-        b_copy(i, False).wait_send()
+    run(0, steps - 2, second)
+    project(0)
+    run(steps - 2, steps - 1, second)
+    project(1)
+    run(steps - 1, steps, second)
+    run(0, steps, third)
+
+    for part in range(2):
+        for i in range(NZ - 1):
+            b_copy(i, part, True).wait_recv()
+    bout[...] = ball[...].reshape(rows, depth)
+
+    for part in range(2):
+        for i in range(NZ - 1):
+            u_copy(i, part, False).wait_send()
+            b_copy(i, part, False).wait_send()
     for t in range(steps - 3, steps):
         g_copy(t).wait_send()
 
@@ -486,10 +498,10 @@
     vm = pltpu.VMEM
     anyspec = pl.BlockSpec(memory_space=pl.ANY)
     vspec = pl.BlockSpec(memory_space=pltpu.VMEM)
-    return pl.pallas_call(
+    code, proto = pl.pallas_call(
         functools.partial(kernel, crops_all, protos_all),
         out_shape=(
-            jax.ShapeDtypeStruct((rows, depth), F32),
+            jax.ShapeDtypeStruct((rows, depth), BF16),
             jax.ShapeDtypeStruct((8, width), F32),
         ),
         in_specs=[anyspec] * 4,
@@ -546,16 +558,30 @@
             dma((steps, 2, 4)),
             dma((steps, 2, 4)),
             dma((steps, 2, 4)),
-            dma((NZ,)),
-            dma((NZ,)),
-            dma((NZ,)),
-            dma((NZ,)),
+            dma((2, NZ)),
+            dma((2, NZ)),
+            dma((2, NZ)),
+            dma((2, NZ)),
         ],
         compiler_params=pltpu.CompilerParams(
             collective_id=0, has_side_effects=True, vmem_limit_bytes=62 * 1024 * 1024
         ),
         name="sinkhorn_head",
     )(teacher_feat, student_feat, teacher_protos, student_protos)
+    return pl.pallas_call(
+        closing,
+        out_shape=(jax.ShapeDtypeStruct((rows, depth), F32), jax.ShapeDtypeStruct((8, width), F32)),
+        in_specs=[vspec] * 3,
+        out_specs=(vspec, vspec),
+        name="closing",
+    )(code, student_feat, proto)
+
+
+def closing(code, feat, proto, bout, pout):
+    s32 = feat[...].astype(F32)
+    norm = jnp.sqrt(jnp.sum(s32 * s32, axis=-1, keepdims=True) + EPS)
+    bout[...] = decode(code[...], 7) / norm
+    pout[...] = proto[...]
 
 
 def solution(mesh):

time: 95.7 us -> 87.2 us (0.911)
  Pallas kernels: 91.4 us -> 86.2 us
  local copies, waits for them, and re-layouts: 3.54 us -> 0 us
    pallas_call x1, Pallas kernels: 91.4 us -> 84 us  [body(): pl.pallas_call(functools.partial(kernel, crops_all, protos_all), out_shap...]
    unnamed x2 -> x0, local copies, waits for them, and re-layouts: 3.54 us -> none
    pallas_call x0 -> x1, Pallas kernels: none -> 2.24 us  [body(): pl.pallas_call(closing, out_shape=(jax.ShapeDtypeStruct((rows, depth), F3...]
where the time goes in v3:
time: 87.2 us; the launch traced here: 86.9 us
  Pallas kernels  86.2 us (99%)
    pallas_call x1, Pallas kernels, body(): pl.pallas_call(functools.partial(kernel, crops_all, protos_all), out_shap...  84 us
    pallas_call x1, Pallas kernels, body(): pl.pallas_call(closing, out_shape=(jax.ShapeDtypeStruct((rows, depth), F3...  2.24 us

profile of v3, /device:TPU:1, one launch (start us, length us, event | category | flops | bytes accessed | tf_op | source)
XLA Modules:
  0.0 86.9 jit_solution(12808831907863042937)
XLA Ops:
  0.6 84.0 %sinkhorn_head.1 = (bf16[512,256]{1,0:T(8,128)(2,1)}, f32[8,8192]{1,0:T(8,128)}) custom-call(bf16[512,256]{1,0:T(8,128)(2,1)} %tf_hbm.1, bf16[512,256]{1,0:T(8,128)(2,1)} %feat.1, bf16[256,8192]{1,0:T(8,128)(2,1)} %tw_hbm.1, bf16[256,8192]{1,0:T(8,128)(2,1)} %sw_hbm.1), custom_call_target="tpu_custom_call" | custom-call | tf_op jit(solution)/shard_map/sinkhorn_head/pallas_call | solution.py:501
  84.6 2.2 %closing.1 = (f32[512,256]{1,0:T(8,128)}, f32[8,8192]{1,0:T(8,128)}) custom-call(bf16[512,256]{1,0:T(8,128)(2,1)} %get-tuple-element.4.code, bf16[512,256]{1,0:T(8,128)(2,1)} %feat.1, f32[8,8192]{1,0:T(8,128)} %get-tuple-element.5.proto), custom_call_target="tpu_custom_call" | custom-call | tf_op jit(solution)/shard_map/closing/pallas_call | solution.py:571

commit v4 on v3

--- a/solution.py
+++ b/solution.py
@@ -24,6 +24,9 @@
 BLOCK = 512
 FINE = 256
 PART = 32
+EARLY = 5
+LAG = 2
+FAR_FIRST = (10, 9, 11, 6, 14, 2, 8, 5, 7, 13, 15, 1, 3, 4, 12)
 
 
 def encode(v, power):
@@ -124,7 +127,7 @@
 
     mate = at(x, y, 1 - core)
     chip_peers = []
-    for k in range(1, CHIPS):
+    for k in FAR_FIRST:
         px, py = lax.rem(x + k // NY, NX), lax.rem(y + k % NY, NY)
         chip_peers.append((px * NY + py, at(px, py, core)))
     z_peers = [lax.rem(z + k, NZ) for k in (4, 3, 5, 2, 6, 1, 7)]
@@ -336,15 +339,20 @@
             hold2.at[t, h, p], land2.at[t, h, q], l2_send.at[t, h, k], l2_recv.at[t, h, q], dev, MESH
         )
 
-    def compute(t):
-        turn = sturn[...].reshape(depth, rows)
+    def partial(t, o, score):
         slot = lax.rem(t, 3)
+        g = jnp.dot(sturn[...].reshape(depth, rows), score, preferred_element_type=F32)
+        gsend[slot, :, o : o + FINE] = g[: depth // 2]
+        gown[slot, :, o : o + FINE] = g[depth // 2 :]
+
+    def compute(t, early):
         unit = None
         here = place(t)
-
-        @pl.when(t >= 3)
-        def _():
-            g_copy(t).wait_send()
+        if early:
+
+            @pl.when(t >= 3)
+            def _():
+                g_copy(t).wait_send()
 
         for o in range(0, W, FINE):
             blocks = []
@@ -357,13 +365,23 @@
                     line.append((sexp[rs, cs] * ascale[rs, :] - tgt * bscale[rs, :]).astype(BF16))
                 blocks.append(jnp.concatenate(line, axis=1))
             score = jnp.concatenate(blocks, axis=0)
-            g = jnp.dot(turn, score, preferred_element_type=F32)
-            gsend[slot, :, o : o + FINE] = g[: depth // 2]
-            gown[slot, :, o : o + FINE] = g[depth // 2 :]
             cols = pl.ds(pl.multiple_of(here * W + o, FINE), FINE)
+            if early:
+                partial(t, o, score)
+            else:
+                expo[:, cols] = score.astype(F32)
             part = jnp.dot(score, swt[cols, :], preferred_element_type=F32)
             unit = part if unit is None else unit + part
         unit_acc[...] += unit
+        if early:
+            g_copy(t).start()
+
+    def late(t):
+        g_copy(t).wait_send()
+        here = place(t)
+        for o in range(0, W, FINE):
+            cols = pl.ds(pl.multiple_of(here * W + o, FINE), FINE)
+            partial(t, o, expo[:, cols].astype(BF16))
         g_copy(t).start()
 
     def first(t):
@@ -378,7 +396,7 @@
         for j in range(NY):
             tw[hold(t, 1, j)] = encode(swap[:, j], 5).reshape(NX * 8, hw)
         for h in range(2):
-            for k in range(1, 4):
+            for k in (2, 1, 3):
                 l1_copy(t, h, k, False).start()
 
     def second(t):
@@ -396,7 +414,7 @@
             for i in range(4):
                 v = total[i]
                 hold2[t, h, i] = encode(jnp.concatenate([v[:, : hw // 2], v[:, hw // 2 :]], axis=0), 5)
-            for k in range(1, 4):
+            for k in (2, 1, 3):
                 l2_copy(t, h, k, False).start()
 
     def third(t):
@@ -437,15 +455,6 @@
             b_copy(i, part, False).start()
         ball[z, own] = bres[own]
 
-    def step(t, _):
-        compute(t)
-
-        @pl.when(t >= 2)
-        def _():
-            first(t - 2)
-
-        return 0
-
     def run(lo, hi, fn):
         def one(t, _):
             fn(t)
@@ -453,17 +462,40 @@
 
         lax.fori_loop(lo, hi, one, 0)
 
-    lax.fori_loop(0, steps, step, 0)
+    def inline(t):
+        compute(t, True)
+
+        @pl.when(t >= LAG)
+        def _():
+            first(t - LAG)
+
+    def after(t):
+        compute(t, False)
+
+        @pl.when(t < EARLY + LAG)
+        def _():
+            first(t - LAG)
+
+    def later(t):
+        late(t)
+
+        @pl.when(t >= EARLY + LAG)
+        def _():
+            first(t - LAG)
+
+    run(0, EARLY, inline)
+    run(EARLY, steps, after)
     unit_out[...] = encode(unit_acc[...], 7).reshape(NZ, rows // NZ, depth)
     for part in range(2):
         for i in range(NZ - 1):
             u_copy(i, part, False).start()
-    run(steps - 2, steps, first)
-    run(0, steps - 2, second)
+    run(EARLY, steps, later)
+    run(steps - LAG, steps, first)
+    run(0, 3, second)
     project(0)
-    run(steps - 2, steps - 1, second)
+    run(3, 4, second)
     project(1)
-    run(steps - 1, steps, second)
+    run(4, steps, second)
     run(0, steps, third)
 
     for part in range(2):

time: 87.2 us -> 84.7 us (0.971)
  Pallas kernels: 86.2 us -> 83.9 us
    pallas_call x1, Pallas kernels: 84 us -> 81.7 us  [body(): pl.pallas_call(functools.partial(kernel, crops_all, protos_all), out_shap...]
where the time goes in v4:
time: 84.7 us; the launch traced here: 84.5 us
  Pallas kernels  83.9 us (99%)
    pallas_call x1, Pallas kernels, body(): pl.pallas_call(functools.partial(kernel, crops_all, protos_all), out_shap...  81.7 us
    pallas_call x1, Pallas kernels, body(): pl.pallas_call(closing, out_shape=(jax.ShapeDtypeStruct((rows, depth), F3...  2.24 us

profile of v4, /device:TPU:1, one launch (start us, length us, event | category | flops | bytes accessed | tf_op | source)
XLA Modules:
  0.0 84.5 jit_solution(5052985483734875477)
XLA Ops:
  0.6 81.7 %sinkhorn_head.1 = (bf16[512,256]{1,0:T(8,128)(2,1)}, f32[8,8192]{1,0:T(8,128)}) custom-call(bf16[512,256]{1,0:T(8,128)(2,1)} %tf_hbm.1, bf16[512,256]{1,0:T(8,128)(2,1)} %feat.1, bf16[256,8192]{1,0:T(8,128)(2,1)} %tw_hbm.1, bf16[256,8192]{1,0:T(8,128)(2,1)} %sw_hbm.1), custom_call_target="tpu_custom_call" | custom-call | tf_op jit(solution)/shard_map/sinkhorn_head/pallas_call | solution.py:533
  82.3 2.2 %closing.1 = (f32[512,256]{1,0:T(8,128)}, f32[8,8192]{1,0:T(8,128)}) custom-call(bf16[512,256]{1,0:T(8,128)(2,1)} %get-tuple-element.4.code, bf16[512,256]{1,0:T(8,128)(2,1)} %feat.1, f32[8,8192]{1,0:T(8,128)} %get-tuple-element.5.proto), custom_call_target="tpu_custom_call" | custom-call | tf_op jit(solution)/shard_map/closing/pallas_call | solution.py:603

commit v5 on v4

--- a/solution.py
+++ b/solution.py
@@ -491,11 +491,11 @@
             u_copy(i, part, False).start()
     run(EARLY, steps, later)
     run(steps - LAG, steps, first)
-    run(0, 3, second)
+    run(0, 5, second)
     project(0)
-    run(3, 4, second)
+    run(5, 6, second)
     project(1)
-    run(4, steps, second)
+    run(6, steps, second)
     run(0, steps, third)
 
     for part in range(2):

time: 84.7 us -> 84.7 us (level)
  no operation moved by 1% of the time
where the time goes in v5:
time: 84.7 us; the launch traced here: 84.5 us
  Pallas kernels  83.9 us (99%)
    pallas_call x1, Pallas kernels, body(): pl.pallas_call(functools.partial(kernel, crops_all, protos_all), out_shap...  81.7 us
    pallas_call x1, Pallas kernels, body(): pl.pallas_call(closing, out_shape=(jax.ShapeDtypeStruct((rows, depth), F3...  2.24 us

profile of v5, /device:TPU:1, one launch (start us, length us, event | category | flops | bytes accessed | tf_op | source)
XLA Modules:
  0.0 84.5 jit_solution(10126909359521338965)
XLA Ops:
  0.6 81.7 %sinkhorn_head.1 = (bf16[512,256]{1,0:T(8,128)(2,1)}, f32[8,8192]{1,0:T(8,128)}) custom-call(bf16[512,256]{1,0:T(8,128)(2,1)} %tf_hbm.1, bf16[512,256]{1,0:T(8,128)(2,1)} %feat.1, bf16[256,8192]{1,0:T(8,128)(2,1)} %tw_hbm.1, bf16[256,8192]{1,0:T(8,128)(2,1)} %sw_hbm.1), custom_call_target="tpu_custom_call" | custom-call | tf_op jit(solution)/shard_map/sinkhorn_head/pallas_call | solution.py:533
  82.3 2.2 %closing.1 = (f32[512,256]{1,0:T(8,128)}, f32[8,8192]{1,0:T(8,128)}) custom-call(bf16[512,256]{1,0:T(8,128)(2,1)} %get-tuple-element.4.code, bf16[512,256]{1,0:T(8,128)(2,1)} %feat.1, f32[8,8192]{1,0:T(8,128)} %get-tuple-element.5.proto), custom_call_target="tpu_custom_call" | custom-call | tf_op jit(solution)/shard_map/closing/pallas_call | solution.py:603
